TPU v7x, 128 devices: a whole 4x4x4 slice. The times are simulated.
128 devices in a mesh: tm: 16 (over y_lo, x, core), head: 8 (over z, y_hi).
Axes of the slice: x: 4, y: 4 (y_hi: 2, y_lo: 2; y = y_hi * 2 + y_lo), z: 4, core: 2. Of those that a mesh axis runs over, the one named last changes fastest.
Arguments:
- queries: bfloat16 [32768, 3072], P('tm', 'head'), may hold values from -8 to 8
- keys: bfloat16 [32768, 3072], P('tm', 'head'), may hold values from -8 to 8
- values: bfloat16 [32768, 3072], P('tm', 'head'), may hold values from -6 to 6
- right_blocks: bfloat16 [24, 128, 128], P('head'), may hold values from -0.5 to 0.5
- left_blocks: bfloat16 [24, 128, 128], P('head'), may hold values from -0.5 to 0.5
- block_perm: int32 [24], replicated, may hold values from 0 to 23, each once
- reach: int32 [24], replicated, may hold values from 0 to 2, as said below
- grad_out: bfloat16 [32768, 3072], P('tm', 'head'), may hold values from -6 to 6
Outputs:
- projected: bfloat16 [32768, 3072], P('tm', 'head')
- d_queries: bfloat16 [32768, 3072], P('tm', 'head')
- d_keys: bfloat16 [32768, 3072], P('tm', 'head')
- d_values: bfloat16 [32768, 3072], P('tm', 'head')
- d_right: float32 [24, 128, 128], P('head')
- d_left: float32 [24, 128, 128], P('head')
Inputs may be any that keep to these rules, and one draw needn't show every extreme that they name: At least one head has reach 2. `block_perm`: each block number once.
All inputs are finite; a program needn't handle non-finite values.
Results may differ from a plain program's by a relative error of at most 0.023.
Values may be sent and summed in bfloat16 or wider, within the bound.
No kernel may reach another device: no remote copies, remote signals or barrier semaphores. Data moves between devices by JAX's collectives and lax.ppermute only.
A program may use at most 192 MiB of HBM per device.

v0:
```python
import jax
import jax.numpy as jnp
from jax import lax
from jax.sharding import PartitionSpec as P

NB = 24
BLK = 128
TILE = 128
RADIUS = 2
FR_DEV = 4
NTILE = 4


def padded(block, sides, width):
    for axis, dim in sides:
        count = lax.axis_size(axis)
        forward = [(i, i + 1) for i in range(count - 1)]
        backward = [(target, source) for source, target in forward]
        low = lax.ppermute(
            lax.slice_in_dim(block, block.shape[dim] - width, None, axis=dim), axis, forward
        )
        high = lax.ppermute(lax.slice_in_dim(block, 0, width, axis=dim), axis, backward)
        block = jnp.concatenate([low, block, high], axis=dim)
    return block


def shifted(x, axis, by):
    size = lax.axis_size(axis)
    pairs = [(i, i + by) for i in range(size) if 0 <= i + by < size]
    return lax.ppermute(x, axis, pairs)


def frame_mask(reach_heads, frames_q, frames_k, total_frames):
    gap = jnp.abs(frames_q[:, None] - frames_k[None, :])
    valid_q = (frames_q >= 0) & (frames_q < total_frames)
    valid_k = (frames_k >= 0) & (frames_k < total_frames)
    inside = valid_q[:, None] & valid_k[None, :]
    return (gap[None, :, :] <= reach_heads[:, None, None]) & inside[None, :, :]


def frame_list(first, count):
    return first + jnp.arange(count * TILE, dtype=jnp.int32) // TILE


def to_tiles(rows_array, local_heads):
    shaped = rows_array.reshape(FR_DEV, NTILE, TILE, local_heads, BLK)
    return jnp.transpose(shaped, (1, 3, 0, 2, 4))


def from_tiles(tiled, local_heads):
    shaped = tiled.reshape(NTILE, local_heads, FR_DEV, TILE, BLK)
    return jnp.transpose(shaped, (2, 0, 3, 1, 4)).reshape(FR_DEV * NTILE * TILE, local_heads * BLK)


def flat_rows(block):
    return block.reshape(block.shape[0], block.shape[1] * block.shape[2], block.shape[3])


def flat_stats(block):
    return block.reshape(block.shape[0], block.shape[1] * block.shape[2])


def scores(q_rows, k_rows, scale):
    return jnp.einsum("hqd,hkd->hqk", q_rows, k_rows, preferred_element_type=jnp.float32) * scale


def attend(q_rows, k_rows, v_rows, allowed, scale):
    s = scores(q_rows, k_rows, scale)
    top = jnp.max(jnp.where(allowed, s, -jnp.inf), axis=2, keepdims=True)
    total = jnp.sum(jnp.where(allowed, jnp.exp(s - top), 0.0), axis=2, keepdims=True)
    lse = top + jnp.log(total)
    probs = jnp.where(allowed, jnp.exp(s - lse), 0.0).astype(jnp.bfloat16)
    out = jnp.einsum("hqk,hkd->hqd", probs, v_rows, preferred_element_type=jnp.float32)
    return (out.astype(jnp.bfloat16), lse[:, :, 0])


def probs_again(q_rows, k_rows, allowed, lse, scale):
    s = scores(q_rows, k_rows, scale)
    return jnp.where(allowed, jnp.exp(s - lse[:, :, None]), 0.0)


def score_grads(probs, d_rows, v_rows, delta, scale):
    dp = jnp.einsum("hqd,hkd->hqk", d_rows, v_rows, preferred_element_type=jnp.float32)
    return (probs * (dp - delta[:, :, None]) * scale).astype(jnp.bfloat16)


def on_device(queries, keys, values, right_blocks, left_blocks, block_perm, reach, grad_out):
    rows, width = queries.shape
    local_heads = width // BLK
    n_head = lax.axis_size("head")
    piece = BLK // n_head
    scale = BLK ** (-0.5)
    span = FR_DEV + 2 * RADIUS
    total_frames = FR_DEV * lax.axis_size("tm")
    frame_base = lax.axis_index("tm") * FR_DEV
    head_reach = lax.dynamic_slice_in_dim(reach, lax.axis_index("head") * local_heads, local_heads)
    q_tiles = to_tiles(queries, local_heads)
    pair = jnp.stack([to_tiles(keys, local_heads), to_tiles(values, local_heads)])
    pair_ext = padded(pair, (("tm", 3),), RADIUS)
    k_ext = pair_ext[0]
    v_ext = pair_ext[1]
    own_frames = frame_list(frame_base, FR_DEV)
    ext_frames = frame_list(frame_base - RADIUS, span)
    near = frame_mask(head_reach, own_frames, ext_frames, total_frames)

    def forward_tile(items):
        q_block, k_block, v_block = items
        return attend(flat_rows(q_block), flat_rows(k_block), flat_rows(v_block), near, scale)

    attn_tiles, lse_tiles = lax.map(forward_tile, (q_tiles, k_ext, v_ext))
    attn_flat = from_tiles(attn_tiles, local_heads)
    attn_rows = attn_flat.reshape(rows, local_heads, BLK)
    columns = jnp.arange(width, dtype=jnp.int32)
    out_block = columns % NB
    out_lane = columns // NB
    picked = jnp.sum(
        jnp.where(
            jnp.arange(NB, dtype=jnp.int32)[None, :] == out_block[:, None], block_perm[None, :], 0
        ),
        axis=1,
    )
    source = picked * piece + out_lane
    placer = (columns[:, None] == source[None, :]).astype(jnp.bfloat16)
    r4 = right_blocks.reshape(local_heads, BLK, n_head, piece)
    mixed = jnp.einsum("nbi,bisl->sbln", attn_rows, r4, preferred_element_type=jnp.float32).astype(
        jnp.bfloat16
    )
    mixed = mixed.reshape(n_head, local_heads * piece, rows)
    arrived = lax.all_to_all(mixed, "head", split_axis=0, concat_axis=0, tiled=True).reshape(
        width, rows
    )
    placed_t = jnp.dot(placer.T, arrived, preferred_element_type=jnp.float32).astype(jnp.bfloat16)
    placed3 = placed_t.reshape(local_heads, BLK, rows)
    projected = jnp.einsum("cin,cio->nco", placed3, left_blocks, preferred_element_type=jnp.float32)
    projected = projected.astype(jnp.bfloat16).reshape(rows, width)
    cot3 = grad_out.reshape(rows, local_heads, BLK)
    d_placed = jnp.einsum(
        "nco,cio->cin", cot3, left_blocks, preferred_element_type=jnp.float32
    ).astype(jnp.bfloat16)
    left_term = jnp.einsum("cin,nco->cio", placed3, cot3, preferred_element_type=jnp.float32)
    d_arrived = jnp.dot(
        placer, d_placed.reshape(width, rows), preferred_element_type=jnp.float32
    ).astype(jnp.bfloat16)
    d_mixed = lax.all_to_all(
        d_arrived.reshape(n_head, local_heads * piece, rows),
        "head",
        split_axis=0,
        concat_axis=0,
        tiled=True,
    )
    d4 = d_mixed.reshape(n_head, local_heads, piece, rows)
    d_attn = jnp.einsum("sbln,bisl->nbi", d4, r4, preferred_element_type=jnp.float32).astype(
        jnp.bfloat16
    )
    right_term = jnp.einsum(
        "nbi,sbln->bisl", attn_rows, d4, preferred_element_type=jnp.float32
    ).reshape(local_heads, BLK, BLK)
    right_sum, left_sum = (
        lax.psum(right_term.astype(jnp.bfloat16), "tm").astype(jnp.float32),
        lax.psum(left_term.astype(jnp.bfloat16), "tm").astype(jnp.float32),
    )
    norm = float(rows * lax.axis_size("tm")) ** (-0.5)
    d_right = right_sum * norm
    d_left = left_sum * norm
    delta = jnp.sum(d_attn.astype(jnp.float32) * attn_rows.astype(jnp.float32), axis=2)
    delta_tiles = jnp.transpose(delta.reshape(FR_DEV, NTILE, TILE, local_heads), (1, 3, 0, 2))
    lse_shaped = lse_tiles.reshape(NTILE, local_heads, FR_DEV, TILE)
    d_tiles = to_tiles(d_attn.reshape(rows, width), local_heads)

    def backward_tile(items):
        q_block, d_block, k_block, v_block, lse_block, delta_block = items
        q_rows = flat_rows(q_block)
        d_rows = flat_rows(d_block)
        k_rows = flat_rows(k_block)
        probs = probs_again(q_rows, k_rows, near, flat_stats(lse_block), scale)
        grads = score_grads(probs, d_rows, flat_rows(v_block), flat_stats(delta_block), scale)
        d_query = jnp.einsum(
            "hqk,hkd->hqd", grads, k_rows, preferred_element_type=jnp.float32
        ).astype(jnp.bfloat16)
        d_key = jnp.einsum("hqk,hqd->hkd", grads, q_rows, preferred_element_type=jnp.float32)
        d_value = jnp.einsum(
            "hqk,hqd->hkd", probs.astype(jnp.bfloat16), d_rows, preferred_element_type=jnp.float32
        )
        return (d_query, jnp.stack([d_key, d_value]))

    dq_tiles, kv_tiles = lax.map(
        backward_tile, (q_tiles, d_tiles, k_ext, v_ext, lse_shaped, delta_tiles)
    )
    kv_grads = kv_tiles.reshape(NTILE, 2, local_heads, span, TILE, BLK)
    from_above = shifted(kv_grads[:, :, :, :RADIUS].astype(jnp.bfloat16), "tm", -1).astype(
        jnp.float32
    )
    from_below = shifted(kv_grads[:, :, :, RADIUS + FR_DEV :].astype(jnp.bfloat16), "tm", 1).astype(
        jnp.float32
    )
    own = kv_grads[:, :, :, RADIUS : RADIUS + FR_DEV]
    own = own.at[:, :, :, FR_DEV - RADIUS :].add(from_above)
    own = own.at[:, :, :, :RADIUS].add(from_below)
    own = own.astype(jnp.bfloat16)
    d_queries = from_tiles(dq_tiles, local_heads)
    d_keys = from_tiles(own[:, 0], local_heads)
    d_values = from_tiles(own[:, 1], local_heads)
    return (projected, d_queries, d_keys, d_values, d_right, d_left)


def solution(mesh):
    in_specs = (
        P("tm", "head"),
        P("tm", "head"),
        P("tm", "head"),
        P("head", None, None),
        P("head", None, None),
        P(),
        P(),
        P("tm", "head"),
    )
    out_specs = (
        P("tm", "head"),
        P("tm", "head"),
        P("tm", "head"),
        P("tm", "head"),
        P("head", None, None),
        P("head", None, None),
    )
    return jax.shard_map(
        on_device, mesh=mesh, in_specs=in_specs, out_specs=out_specs, check_vma=False
    )
```

profile of v0, /device:TPU:7, one launch (start us, length us, event | category | flops | bytes accessed | tf_op | source)
XLA Modules:
  0.0 383.8 jit_solution(6202498669068435902)
XLA Ops:
  10.1 3.1 copy.66
  16.1 3.5 fusion.25
  19.6 3.7 collective-permute-start
  29.8 7.9 %all-to-all-start.1 = ((bf16[8,48,2048]{2,1,0:T(8,128)(2,1)}), bf16[8,48,2048]{2,1,0:T(8,128)(2,1)}, u32[]{:S(2)}, u32[]{:S(2)}) async-start(bf16[8,48,2048]{2,1,0:T(8,128)(2,1)} %bitcast.21), calls=%async_computation.1 | async-start | bytes 3145728 | tf_op jit(solution)/shard_map/all_to_all | solution.py:144
  43.1 4.7 %collective-permute-done.1 = bf16[2,4,3,2,128,128]{4,1,3,5,2,0:T(4,128)(2,1)} collective-permute-done((bf16[2,4,3,2,128,128]{4,1,3,5,2,0:T(4,128)(2,1)}, bf16[2,4,3,2,128,128]{4,1,3,5,2,0:T(4,128)(2,1)}, u32[]{:S(2)}, u32[]{:S(2)}) %collective-permute-start.1) | collective-permute-done | bytes 1572896 | tf_op jit(solution)/shard_map/ppermute | solution.py:22
  47.8 7.1 %pad_maximum_fusion = bf16[2,4,3,8,128,128]{4,1,3,5,2,0:T(4,128)(2,1)S(1)} fusion(bf16[2,4,3,2,128,128]{4,1,3,5,2,0:T(4,128)(2,1)} %collective-permute-done.1, bf16[1,4,3,4,128,128]{4,1,3,5,2,0:T(4,128)(2,1)} %bitcast.199, bf16[1,4,3,4,128,128]{4,1,3,5,2,0:T(4,128)(2,1)} %bitcast.197, bf16[2,4,3,2,128,128]{4,1,3,5,2,0:T(4,128)(2,1)} %collective-permute-done), kind=kLoop, calls=%fused_computation.40 | loop fusion | flops 9437184 | bytes 12582912 | tf_op jit(solution)/shard_map/concatenate | solution.py:23
  54.8 4.1 %slice_bitcast_fusion = (bf16[4,3,8,128,128]{3,0,2,4,1:T(4,128)(2,1)}, bf16[4,3,8,128,128]{3,0,2,4,1:T(4,128)(2,1)}) fusion(bf16[2,4,3,8,128,128]{4,1,3,5,2,0:T(4,128)(2,1)S(1)} %pad_maximum_fusion), kind=kLoop, calls=%fused_computation.45 | loop fusion | bytes 12582912 | tf_op jit(solution)/shard_map/squeeze | solution.py:101
  59.0 6.2 %copy.69 = bf16[4,3,8,128,128]{4,3,2,1,0:T(8,128)(2,1)} copy(bf16[4,3,8,128,128]{3,0,2,4,1:T(4,128)(2,1)} %get-tuple-element.295) | data formatting | bytes 6291456
  65.2 6.2 %copy.68 = bf16[4,3,8,128,128]{4,3,2,1,0:T(8,128)(2,1)} copy(bf16[4,3,8,128,128]{3,0,2,4,1:T(4,128)(2,1)} %get-tuple-element.296) | data formatting | bytes 6291456
  72.8 42.0 %while.28 = (s32[]{:T(128)}, bf16[4,3,512,128]{3,2,1,0:T(8,128)(2,1)}, f32[4,3,512]{2,1,0:T(4,128)S(1)}, bf16[4,3,4,128,128]{4,3,2,1,0:T(8,128)(2,1)}, bf16[4,3,...) while((s32[]{:T(128)}, ...), condition=%wide.region_4.5_spmd.clone, body=%wide.region_1.4_spmd.clone.sunk | while | flops 832240128 | bytes 33087648 | solution.py:110
  80.1 3.2 fusion.96
  90.6 3.2 fusion.96
  101.1 3.2 fusion.96
  111.5 3.2 fusion.96
  117.5 3.8 multiply_reduce_fusion
  126.3 7.2 %all-to-all-start = ((bf16[8,48,2048]{2,1,0:T(8,128)(2,1)}), bf16[8,48,2048]{2,1,0:T(8,128)(2,1)}, u32[]{:S(2)}, u32[]{:S(2)}) async-start(bf16[8,48,2048]{2,1,0:T(8,128)(2,1)} %bitcast.206), calls=%async_computation | async-start | bytes 3145728 | tf_op jit(solution)/shard_map/all_to_all | solution.py:129
  133.5 10.3 %all-reduce.3.cloned.1.call-start = ((), (), s32[]{:S(2)}) async-start(), calls=%async_computation.2 | async-start | bytes 393216 | tf_op jit(solution)/shard_map/psum | solution.py:159
  145.2 56.8 %while.29 = (s32[]{:T(128)}, bf16[4,3,512,128]{3,2,1,0:T(8,128)(2,1)}, f32[4,2,3,1024,128]{4,3,2,1,0:T(8,128)}, bf16[4,3,4,128,128]{4,3,2,1,0:T(8,128)(2,1)}, bf...) while((s32[]{:T(128)}, ...), condition=%wide.region_7.8_spmd.clone, body=%wide.region_6.7_spmd.clone.sunk | while | flops 2037841920 | bytes 52103348 | solution.py:186
  151.6 3.0 multiply_convert_fusion.2
  165.7 3.0 multiply_convert_fusion.2
  179.9 3.0 multiply_convert_fusion.2
  194.2 3.0 multiply_convert_fusion.2
  202.1 15.1 %copy.85 = f32[4,2,3,8,128,128]{4,0,3,5,2,1:T(4,128)} copy(f32[4,2,3,8,128,128]{5,4,3,2,1,0:T(8,128)} %bitcast.200) | data formatting | bytes 25165824 | tf_op jit(solution)/shard_map/reshape | solution.py:189
  217.2 10.4 %convert.4 = bf16[4,2,3,8,128,128]{4,0,3,5,2,1:T(4,128)(2,1)} convert(f32[4,2,3,8,128,128]{4,0,3,5,2,1:T(4,128)} %copy.85) | non-fusion elementwise | flops 3145728 | bytes 18874368 | tf_op jit(solution)/shard_map/convert.1
  227.6 4.9 %fusion.48 = (bf16[4,2,3,2,128,128]{4,0,3,5,2,1:T(4,128)(2,1)}, bf16[4,2,3,2,128,128]{4,0,3,5,2,1:T(4,128)(2,1)}) fusion(bf16[4,2,3,8,128,128]{4,0,3,5,2,1:T(4,128)(2,1)} %convert.4), kind=kLoop, calls=%fused_computation.104 | loop fusion | bytes 6291456 | tf_op jit(solution)/shard_map/slice | solution.py:193
  234.5 6.7 %slice.123 = f32[4,2,3,4,128,128]{4,0,3,5,2,1:T(4,128)} slice(f32[4,2,3,8,128,128]{4,0,3,5,2,1:T(4,128)} %copy.85), slice={[0:4], [0:2], [0:3], [2:6], [0:128], [0:128]} | slice | bytes 12582912 | tf_op jit(solution)/shard_map/slice | solution.py:196
  241.1 5.7 %collective-permute-start.3 = (bf16[4,2,3,2,128,128]{4,0,3,5,2,1:T(4,128)(2,1)}, bf16[4,2,3,2,128,128]{4,0,3,5,2,1:T(4,128)(2,1)}, u32[]{:S(2)}, u32[]{:S(2)}) collective-permute-start(bf16[4,2,3,2,128,128]{4,0,3,5,2,1:T(4,128)(2,1)} %get-tuple-element.293), channel_id=1, source_target_pairs={{0,8},{8,16},{16,24},{24,32},{32,40},{40,48},{48,56},{56,64},{64,7... | collective-permute-start | bytes 4718600 | tf_op jit(solution)/shard_map/ppermute | solution.py:30
  262.2 4.9 %fusion.24 = f32[4,2,3,4,128,128]{4,0,3,5,2,1:T(4,128)} fusion(f32[4,2,3,4,128,128]{4,0,3,5,2,1:T(4,128)} %slice.123, f32[4,2,3,8,128,128]{4,0,3,5,2,1:T(4,128)} %copy.85, bf16[4,2,3,2,128,128]{4,0,3,5,2,1:T(4,128)(2,1)} %collective-permute-done.2), kind=kLoop, calls=%fused_computation.44 | loop fusion | flops 1572864 | bytes 7864320 | tf_op jit(solution)/shard_map/scatter-add | solution.py:197
  267.1 4.9 %fusion.23 = f32[4,2,3,4,128,128]{4,0,3,5,2,1:T(4,128)} fusion(f32[4,2,3,4,128,128]{4,0,3,5,2,1:T(4,128)} %fusion.24, bf16[4,2,3,2,128,128]{4,0,3,5,2,1:T(4,128)(2,1)} %collective-permute-done.3), kind=kLoop, calls=%fused_computation.42 | loop fusion | flops 1572864 | bytes 7864320 | tf_op jit(solution)/shard_map/scatter-add | solution.py:198
  271.9 3.9 %convert_element_type.88 = bf16[4,2,3,4,128,128]{4,0,3,5,2,1:T(4,128)(2,1)S(1)} convert(f32[4,2,3,4,128,128]{4,0,3,5,2,1:T(4,128)} %fusion.23) | non-fusion elementwise | flops 1572864 | bytes 9437184 | tf_op jit(solution)/shard_map/convert_element_type | solution.py:199
  278.0 2.9 reshape.364
  285.2 89.8 %all-reduce.3.cloned.1.call-done = (bf16[3,128,128]{2,1,0:T(8,128)(2,1)}, bf16[3,128,128]{2,1,0:T(8,128)(2,1)}) async-done(((bf16[3,128,128]{2,1,0:T(8,128)(2,1)}, bf16[3,128,128]{2,1,0:T(8,128)(2,1)}), (bf16[3,128,128]{2,1,0:T(8,128)(2,1)}, bf16[3,128,128]{2,1,0:T(8,128)(2,1)})) %all-reduce.3.cloned.1.call-update) | async-done | bytes 196624 | tf_op jit(solution)/shard_map/psum | solution.py:159
  (141 shorter events, 127.1 us)
Async XLA Ops:
  7.2 19.9 %copy-start = (bf16[3,128,128]{2,1,0:T(8,128)(2,1)S(1)}, bf16[3,128,128]{2,1,0:T(8,128)(2,1)}, u32[]{:S(2)}) copy-start(bf16[3,128,128]{2,1,0:T(8,128)(2,1)} %param.20) | copy-start | bytes 294916
  10.1 6.0 %copy-start.3 = (bf16[4,4,128,3,128]{2,1,0,4,3:T(4,128)(2,1)}, bf16[4,4,128,3,128]{2,1,0,4,3:T(4,128)(2,1)S(1)}, u32[]{:S(2)}) copy-start(bf16[4,4,128,3,128]{2,1,0,4,3:T(4,128)(2,1)S(1)} %reshape.346) | copy-start | bytes 4718596
  16.1 3.5 copy-start.4
  16.1 9.1 %copy-start.12 = (s32[24]{0:T(128)S(1)}, s32[24]{0:T(128)}, u32[]{:S(2)}) copy-start(s32[24]{0:T(128)} %param.21) | copy-start | bytes 292
  19.6 23.5 %collective-permute-start = (bf16[2,4,3,2,128,128]{4,1,3,5,2,0:T(4,128)(2,1)}, bf16[2,4,3,2,128,128]{4,1,3,5,2,0:T(4,128)(2,1)}, u32[]{:S(2)}, u32[]{:S(2)}) collective-permute-start(bf16[2,4,3,2,128,128]{4,1,3,5,2,0:T(4,128)(2,1)} %get-tuple-element.299), channel_id=1, source_target_pairs={{0,8},{8,16},{16,24},{24,32},{32,40},{40,48},{48,56},{56,64},{64,7... | collective-permute-start | bytes 4718600 | tf_op jit(solution)/shard_map/ppermute | solution.py:19
  23.3 24.5 %collective-permute-start.1 = (bf16[2,4,3,2,128,128]{4,1,3,5,2,0:T(4,128)(2,1)}, bf16[2,4,3,2,128,128]{4,1,3,5,2,0:T(4,128)(2,1)}, u32[]{:S(2)}, u32[]{:S(2)}) collective-permute-start(bf16[2,4,3,2,128,128]{4,1,3,5,2,0:T(4,128)(2,1)} %get-tuple-element.300), channel_id=1, source_target_pairs={{8,0},{16,8},{24,16},{32,24},{40,32},{48,40},{56,48},{64,56},{72,6... | collective-permute-start | bytes 4718600 | tf_op jit(solution)/shard_map/ppermute | solution.py:22
  25.3 2.3 copy-start.10
  27.1 2.8 copy-start.1
  29.8 8.0 %copy-start.9 = (bf16[3,128,128]{2,1,0:T(8,128)(2,1)S(1)}, bf16[3,128,128]{2,1,0:T(8,128)(2,1)}, u32[]{:S(2)}) copy-start(bf16[3,128,128]{2,1,0:T(8,128)(2,1)} %param.19) | copy-start | bytes 294916
  29.8 8.1 %copy-start.8 = (bf16[2048,384]{1,0:T(8,128)(2,1)S(1)}, bf16[2048,384]{1,0:T(8,128)(2,1)}, u32[]{:S(2)}) copy-start(bf16[2048,384]{1,0:T(8,128)(2,1)} %param.16) | copy-start | bytes 4718596
  29.8 87.7 %all-to-all-start.1 = ((bf16[8,48,2048]{2,1,0:T(8,128)(2,1)}), bf16[8,48,2048]{2,1,0:T(8,128)(2,1)}, u32[]{:S(2)}, u32[]{:S(2)}) async-start(bf16[8,48,2048]{2,1,0:T(8,128)(2,1)} %bitcast.21), calls=%async_computation.1 | async-start | bytes 3145728 | tf_op jit(solution)/shard_map/all_to_all | solution.py:144
  39.8 2.5 copy-start.13
  121.4 2.9 copy-start.6
  126.3 127.7 %all-to-all-start = ((bf16[8,48,2048]{2,1,0:T(8,128)(2,1)}), bf16[8,48,2048]{2,1,0:T(8,128)(2,1)}, u32[]{:S(2)}, u32[]{:S(2)}) async-start(bf16[8,48,2048]{2,1,0:T(8,128)(2,1)} %bitcast.206), calls=%async_computation | async-start | bytes 3145728 | tf_op jit(solution)/shard_map/all_to_all | solution.py:129
  133.5 241.5 %all-reduce.3.cloned.1.call-start = ((), (), s32[]{:S(2)}) async-start(), calls=%async_computation.2 | async-start | bytes 393216 | tf_op jit(solution)/shard_map/psum | solution.py:159
  232.4 14.5 %copy-start.7 = (bf16[4,3,4,128,128]{4,3,0,2,1:T(8,128)(2,1)S(1)}, bf16[4,3,4,128,128]{4,3,0,2,1:T(8,128)(2,1)}, u32[]{:S(2)}) copy-start(bf16[4,3,4,128,128]{4,3,0,2,1:T(8,128)(2,1)} %copy.70) | copy-start | bytes 4718596
  232.4 29.8 %collective-permute-start.2 = (bf16[4,2,3,2,128,128]{4,0,3,5,2,1:T(4,128)(2,1)}, bf16[4,2,3,2,128,128]{4,0,3,5,2,1:T(4,128)(2,1)}, u32[]{:S(2)}, u32[]{:S(2)}) collective-permute-start(bf16[4,2,3,2,128,128]{4,0,3,5,2,1:T(4,128)(2,1)} %get-tuple-element.294), channel_id=1, source_target_pairs={{8,0},{16,8},{24,16},{32,24},{40,32},{48,40},{56,48},{64,56},{72,6... | collective-permute-start | bytes 4718600 | tf_op jit(solution)/shard_map/ppermute | solution.py:30
  241.1 25.9 %collective-permute-start.3 = (bf16[4,2,3,2,128,128]{4,0,3,5,2,1:T(4,128)(2,1)}, bf16[4,2,3,2,128,128]{4,0,3,5,2,1:T(4,128)(2,1)}, u32[]{:S(2)}, u32[]{:S(2)}) collective-permute-start(bf16[4,2,3,2,128,128]{4,0,3,5,2,1:T(4,128)(2,1)} %get-tuple-element.293), channel_id=1, source_target_pairs={{0,8},{8,16},{16,24},{24,32},{32,40},{40,48},{48,56},{56,64},{64,7... | collective-permute-start | bytes 4718600 | tf_op jit(solution)/shard_map/ppermute | solution.py:30
  246.9 2.9 copy-start.5
  252.4 1.6 copy-start.11
  258.2 2.7 copy-start.2
Sparse Core Ops, SparseCore 0:
  262.3 112.6 all-reduce.2
where the time goes:
time: 390 us; the launch traced here: 384 us
  local copies, waits for them, and re-layouts  106 us (27%)
  waiting for transfers between devices  94.5 us (24%)
  matrix products  74.1 us (19%)
  other arithmetic  55.6 us (14%)
  starting transfers between devices  38.8 us (10%)
  between operations  14.7 us (4%)
    psum x1, waiting for transfers between devices, on_device(): lax.psum(right_term.astype(jnp.bfloat16), 'tm').astype(jnp.float32)  89.8 us
    unnamed x40, local copies, waits for them, and re-layouts  29.9 us
    dynamic_slice x16, local copies, waits for them, and re-layouts, on_device(): attn_tiles, lse_tiles = lax.map(forward_tile, (q_tiles, k_ext, v_ext))  20.6 us
    reshape x1, local copies, waits for them, and re-layouts, on_device(): kv_grads = kv_tiles.reshape(NTILE, 2, local_heads, span, TILE, BLK)  15.1 us
    dot_general x4, matrix products, attend(): jnp.einsum('hqk,hkd->hqd', probs, v_rows, preferred_element_type=jnp.floa...  12.9 us
    dot_general x8, matrix products, scores(): jnp.einsum('hqd,hkd->hqk', q_rows, k_rows, preferred_element_type=jnp.flo...  12.1 us
    dot_general x4, matrix products, score_grads(): jnp.einsum('hqd,hkd->hqk', d_rows, v_rows, preferred_element_type=jnp.flo...  12 us
    reduce_sum x4, other arithmetic, attend(): jnp.sum(jnp.where(allowed, jnp.exp(s - top), 0.0), axis=2, keepdims=True)  10.7 us
  transfers between devices with their start and end apart: 7, of which 2 were waited for; matrix products, arithmetic and copies ran while one was open for 55% of the time, Pallas kernels for 0%

commit v1 on v0

--- a/solution.py
+++ b/solution.py
@@ -156,7 +156,7 @@
         "nbi,sbln->bisl", attn_rows, d4, preferred_element_type=jnp.float32
     ).reshape(local_heads, BLK, BLK)
     right_sum, left_sum = (
-        lax.psum(right_term.astype(jnp.bfloat16), "tm").astype(jnp.float32),
+        jnp.sum(lax.all_gather(right_term.astype(jnp.bfloat16), "tm"), axis=0).astype(jnp.float32),
         lax.psum(left_term.astype(jnp.bfloat16), "tm").astype(jnp.float32),
     )
     norm = float(rows * lax.axis_size("tm")) ** (-0.5)

time: 390 us -> 371 us (0.951)
  the two profiles are of different devices: /device:TPU:7 before, /device:TPU:1 now
where the time goes in v1:
time: 371 us; the launch traced here: 365 us
  local copies, waits for them, and re-layouts  107 us (29%)
  matrix products  73.5 us (20%)
  waiting for transfers between devices  72.7 us (20%)
  other arithmetic  57.8 us (16%)
  starting transfers between devices  38.7 us (10%)
  between operations  14.7 us (4%)
    psum x1, waiting for transfers between devices, on_device(): lax.psum(left_term.astype(jnp.bfloat16), 'tm').astype(jnp.float32)  56.9 us
    unnamed x38, local copies, waits for them, and re-layouts  28.7 us
    dynamic_slice x16, local copies, waits for them, and re-layouts, on_device(): attn_tiles, lse_tiles = lax.map(forward_tile, (q_tiles, k_ext, v_ext))  20.6 us
    reshape x1, local copies, waits for them, and re-layouts, on_device(): kv_grads = kv_tiles.reshape(NTILE, 2, local_heads, span, TILE, BLK)  15.1 us
    all_gather x1, waiting for transfers between devices, on_device(): lax.all_gather(right_term.astype(jnp.bfloat16), 'tm')  13.5 us
    dot_general x4, matrix products, attend(): jnp.einsum('hqk,hkd->hqd', probs, v_rows, preferred_element_type=jnp.floa...  12.9 us
    dot_general x8, matrix products, scores(): jnp.einsum('hqd,hkd->hqk', q_rows, k_rows, preferred_element_type=jnp.flo...  12.1 us
    dot_general x4, matrix products, score_grads(): jnp.einsum('hqd,hkd->hqk', d_rows, v_rows, preferred_element_type=jnp.flo...  12 us
  transfers between devices with their start and end apart: 8, of which 3 were waited for; matrix products, arithmetic and copies ran while one was open for 58% of the time, Pallas kernels for 0%

profile of v1, /device:TPU:1, one launch (start us, length us, event | category | flops | bytes accessed | tf_op | source)
XLA Modules:
  0.0 365.0 jit_solution(11225482259938510106)
XLA Ops:
  10.1 3.1 copy.99
  16.1 3.5 fusion.25
  19.6 4.5 %collective-permute-start = (bf16[2,4,3,2,128,128]{4,1,3,5,2,0:T(4,128)(2,1)}, bf16[2,4,3,2,128,128]{4,1,3,5,2,0:T(4,128)(2,1)}, u32[]{:S(2)}, u32[]{:S(2)}) collective-permute-start(bf16[2,4,3,2,128,128]{4,1,3,5,2,0:T(4,128)(2,1)} %get-tuple-element.324), channel_id=1, source_target_pairs={{0,8},{8,16},{16,24},{24,32},{32,40},{40,48},{48,56},{56,64},{64,7... | collective-permute-start | bytes 4718600 | tf_op jit(solution)/shard_map/ppermute | solution.py:19
  30.7 8.2 %all-to-all-start.1 = ((bf16[8,48,2048]{2,1,0:T(8,128)(2,1)}), bf16[8,48,2048]{2,1,0:T(8,128)(2,1)}, u32[]{:S(2)}, u32[]{:S(2)}) async-start(bf16[8,48,2048]{2,1,0:T(8,128)(2,1)} %bitcast.21), calls=%async_computation.1 | async-start | bytes 3145728 | tf_op jit(solution)/shard_map/all_to_all | solution.py:144
  46.5 7.1 %pad_maximum_fusion = bf16[2,4,3,8,128,128]{4,1,3,5,2,0:T(4,128)(2,1)S(1)} fusion(bf16[2,4,3,2,128,128]{4,1,3,5,2,0:T(4,128)(2,1)} %collective-permute-done.1, bf16[1,4,3,4,128,128]{4,1,3,5,2,0:T(4,128)(2,1)} %bitcast.199, bf16[1,4,3,4,128,128]{4,1,3,5,2,0:T(4,128)(2,1)} %bitcast.197, bf16[2,4,3,2,128,128]{4,1,3,5,2,0:T(4,128)(2,1)} %collective-permute-done), kind=kLoop, calls=%fused_computation.40 | loop fusion | flops 9437184 | bytes 12582912 | tf_op jit(solution)/shard_map/concatenate | solution.py:23
  53.5 4.1 %slice_bitcast_fusion = (bf16[4,3,8,128,128]{3,0,2,4,1:T(4,128)(2,1)}, bf16[4,3,8,128,128]{3,0,2,4,1:T(4,128)(2,1)}) fusion(bf16[2,4,3,8,128,128]{4,1,3,5,2,0:T(4,128)(2,1)S(1)} %pad_maximum_fusion), kind=kLoop, calls=%fused_computation.45 | loop fusion | bytes 12582912 | tf_op jit(solution)/shard_map/squeeze | solution.py:101
  57.6 6.2 %copy.102 = bf16[4,3,8,128,128]{4,3,2,1,0:T(8,128)(2,1)} copy(bf16[4,3,8,128,128]{3,0,2,4,1:T(4,128)(2,1)} %get-tuple-element.320) | data formatting | bytes 6291456
  63.8 6.2 %copy.101 = bf16[4,3,8,128,128]{4,3,2,1,0:T(8,128)(2,1)} copy(bf16[4,3,8,128,128]{3,0,2,4,1:T(4,128)(2,1)} %get-tuple-element.321) | data formatting | bytes 6291456
  71.4 42.0 %while.28 = (s32[]{:T(128)}, bf16[4,3,512,128]{3,2,1,0:T(8,128)(2,1)}, f32[4,3,512]{2,1,0:T(4,128)S(1)}, bf16[4,3,4,128,128]{4,3,2,1,0:T(8,128)(2,1)}, bf16[4,3,...) while((s32[]{:T(128)}, ...), condition=%wide.region_4.5_spmd.clone, body=%wide.region_1.4_spmd.clone.sunk | while | flops 832240128 | bytes 33087648 | solution.py:110
  78.7 3.2 fusion.96
  89.2 3.2 fusion.96
  99.7 3.2 fusion.96
  110.1 3.2 fusion.96
  116.1 3.8 %multiply_reduce_fusion = (f32[2048,3]{0,1:T(4,128)S(1)}, bf16[3,2048,128]{2,1,0:T(8,128)(2,1)}) fusion(bf16[4,3,4,128,128]{4,3,0,2,1:T(8,128)(2,1)} %copy.103, bf16[8,3,16,2048]{3,2,1,0:T(8,128)(2,1)} %bitcast.22, bf16[3,128,8,16]{1,3,2,0:T(8,128)(2,1)S(1)} %bitcast.220), kind=kOutput, calls=%fused_computation.50 | convolution fusion | flops 205252608 | bytes 4841472 | tf_op jit(solution)/shard_map/sbln,bisl->nbi/dot_general | solution.py:152
  125.0 7.7 %all-to-all-start = ((bf16[8,48,2048]{2,1,0:T(8,128)(2,1)}), bf16[8,48,2048]{2,1,0:T(8,128)(2,1)}, u32[]{:S(2)}, u32[]{:S(2)}) async-start(bf16[8,48,2048]{2,1,0:T(8,128)(2,1)} %bitcast.206), calls=%async_computation | async-start | bytes 3145728 | tf_op jit(solution)/shard_map/all_to_all | solution.py:129
  132.6 10.5 %all-reduce.2.cloned.1.call-start = ((), (), s32[]{:S(2)}) async-start(), calls=%async_computation.3 | async-start | bytes 196608 | tf_op jit(solution)/shard_map/psum | solution.py:160
  144.5 56.8 %while.29 = (s32[]{:T(128)}, bf16[4,3,512,128]{3,2,1,0:T(8,128)(2,1)}, f32[4,2,3,1024,128]{4,3,2,1,0:T(8,128)}, bf16[4,3,4,128,128]{4,3,2,1,0:T(8,128)(2,1)}, bf...) while((s32[]{:T(128)}, ...), condition=%wide.region_7.8_spmd.clone, body=%wide.region_6.7_spmd.clone.sunk | while | flops 2037841920 | bytes 52103348 | solution.py:186
  150.8 3.0 multiply_convert_fusion.2
  165.0 3.0 multiply_convert_fusion.2
  179.2 3.0 multiply_convert_fusion.2
  193.5 3.0 multiply_convert_fusion.2
  208.4 15.1 %copy.118 = f32[4,2,3,8,128,128]{4,0,3,5,2,1:T(4,128)} copy(f32[4,2,3,8,128,128]{5,4,3,2,1,0:T(8,128)} %bitcast.200) | data formatting | bytes 25165824 | tf_op jit(solution)/shard_map/reshape | solution.py:189
  223.5 10.4 %convert.5 = bf16[4,2,3,8,128,128]{4,0,3,5,2,1:T(4,128)(2,1)} convert(f32[4,2,3,8,128,128]{4,0,3,5,2,1:T(4,128)} %copy.118) | non-fusion elementwise | flops 3145728 | bytes 18874368 | tf_op jit(solution)/shard_map/convert.2
  234.0 4.9 %fusion.48 = (bf16[4,2,3,2,128,128]{4,0,3,5,2,1:T(4,128)(2,1)}, bf16[4,2,3,2,128,128]{4,0,3,5,2,1:T(4,128)(2,1)}) fusion(bf16[4,2,3,8,128,128]{4,0,3,5,2,1:T(4,128)(2,1)} %convert.5), kind=kLoop, calls=%fused_computation.104 | loop fusion | bytes 6291456 | tf_op jit(solution)/shard_map/slice | solution.py:193
  240.8 4.0 %collective-permute-start.3 = (bf16[4,2,3,2,128,128]{4,0,3,5,2,1:T(4,128)(2,1)}, bf16[4,2,3,2,128,128]{4,0,3,5,2,1:T(4,128)(2,1)}, u32[]{:S(2)}, u32[]{:S(2)}) collective-permute-start(bf16[4,2,3,2,128,128]{4,0,3,5,2,1:T(4,128)(2,1)} %get-tuple-element.318), channel_id=1, source_target_pairs={{0,8},{8,16},{16,24},{24,32},{32,40},{40,48},{48,56},{56,64},{64,7... | collective-permute-start | bytes 4718600 | tf_op jit(solution)/shard_map/ppermute | solution.py:30
  244.8 6.7 %slice.123 = f32[4,2,3,4,128,128]{4,0,3,5,2,1:T(4,128)} slice(f32[4,2,3,8,128,128]{4,0,3,5,2,1:T(4,128)} %copy.118), slice={[0:4], [0:2], [0:3], [2:6], [0:128], [0:128]} | slice | bytes 12582912 | tf_op jit(solution)/shard_map/slice | solution.py:196
  260.5 56.9 %all-reduce.2.cloned.1.call-done = bf16[3,128,128]{2,1,0:T(8,128)(2,1)} async-done(((bf16[3,128,128]{2,1,0:T(8,128)(2,1)}), bf16[3,128,128]{2,1,0:T(8,128)(2,1)}) %all-reduce.2.cloned.1.call-update) | async-done | bytes 98320 | tf_op jit(solution)/shard_map/psum | solution.py:160
  319.0 4.9 %fusion.24 = f32[4,2,3,4,128,128]{4,0,3,5,2,1:T(4,128)} fusion(f32[4,2,3,4,128,128]{4,0,3,5,2,1:T(4,128)} %slice.123, f32[4,2,3,8,128,128]{4,0,3,5,2,1:T(4,128)} %copy.118, bf16[4,2,3,2,128,128]{4,0,3,5,2,1:T(4,128)(2,1)} %collective-permute-done.2), kind=kLoop, calls=%fused_computation.44 | loop fusion | flops 1572864 | bytes 7864320 | tf_op jit(solution)/shard_map/scatter-add | solution.py:197
  323.9 4.8 %fusion.23 = f32[4,2,3,4,128,128]{4,0,3,5,2,1:T(4,128)} fusion(f32[4,2,3,4,128,128]{4,0,3,5,2,1:T(4,128)} %fusion.24, bf16[4,2,3,2,128,128]{4,0,3,5,2,1:T(4,128)(2,1)} %collective-permute-done.3), kind=kLoop, calls=%fused_computation.42 | loop fusion | flops 1572864 | bytes 7864320 | tf_op jit(solution)/shard_map/scatter-add | solution.py:198
  328.7 3.9 %convert_element_type.97 = bf16[4,2,3,4,128,128]{4,0,3,5,2,1:T(4,128)(2,1)S(1)} convert(f32[4,2,3,4,128,128]{4,0,3,5,2,1:T(4,128)} %fusion.23) | non-fusion elementwise | flops 1572864 | bytes 9437184 | tf_op jit(solution)/shard_map/convert_element_type | solution.py:199
  334.8 2.9 reshape.374
  342.1 13.5 %all-gather.2.cloned.1.call-done = bf16[16,3,128,128]{3,2,1,0:T(8,128)(2,1)} async-done(((bf16[1,3,128,128]{3,2,1,0:T(8,128)(2,1)}), bf16[16,3,128,128]{3,2,1,0:T(8,128)(2,1)}) %all-gather.2.cloned.1.call-update) | async-done | bytes 1572880 | tf_op jit(solution)/shard_map/all_gather | solution.py:159
  (144 shorter events, 132.3 us)
Async XLA Ops:
  7.2 20.7 %copy-start = (bf16[3,128,128]{2,1,0:T(8,128)(2,1)S(1)}, bf16[3,128,128]{2,1,0:T(8,128)(2,1)}, u32[]{:S(2)}) copy-start(bf16[3,128,128]{2,1,0:T(8,128)(2,1)} %param.20) | copy-start | bytes 294916
  10.1 6.0 %copy-start.3 = (bf16[4,4,128,3,128]{2,1,0,4,3:T(4,128)(2,1)}, bf16[4,4,128,3,128]{2,1,0,4,3:T(4,128)(2,1)S(1)}, u32[]{:S(2)}) copy-start(bf16[4,4,128,3,128]{2,1,0,4,3:T(4,128)(2,1)S(1)} %reshape.356) | copy-start | bytes 4718596
  16.1 3.5 copy-start.4
  16.1 10.0 %copy-start.11 = (s32[24]{0:T(128)S(1)}, s32[24]{0:T(128)}, u32[]{:S(2)}) copy-start(s32[24]{0:T(128)} %param.21) | copy-start | bytes 292
  19.6 24.7 %collective-permute-start = (bf16[2,4,3,2,128,128]{4,1,3,5,2,0:T(4,128)(2,1)}, bf16[2,4,3,2,128,128]{4,1,3,5,2,0:T(4,128)(2,1)}, u32[]{:S(2)}, u32[]{:S(2)}) collective-permute-start(bf16[2,4,3,2,128,128]{4,1,3,5,2,0:T(4,128)(2,1)} %get-tuple-element.324), channel_id=1, source_target_pairs={{0,8},{8,16},{16,24},{24,32},{32,40},{40,48},{48,56},{56,64},{64,7... | collective-permute-start | bytes 4718600 | tf_op jit(solution)/shard_map/ppermute | solution.py:19
  24.1 22.3 %collective-permute-start.1 = (bf16[2,4,3,2,128,128]{4,1,3,5,2,0:T(4,128)(2,1)}, bf16[2,4,3,2,128,128]{4,1,3,5,2,0:T(4,128)(2,1)}, u32[]{:S(2)}, u32[]{:S(2)}) collective-permute-start(bf16[2,4,3,2,128,128]{4,1,3,5,2,0:T(4,128)(2,1)} %get-tuple-element.325), channel_id=1, source_target_pairs={{8,0},{16,8},{24,16},{32,24},{40,32},{48,40},{56,48},{64,56},{72,6... | collective-permute-start | bytes 4718600 | tf_op jit(solution)/shard_map/ppermute | solution.py:22
  26.2 2.3 copy-start.9
  27.9 2.8 copy-start.1
  30.7 8.3 %copy-start.8 = (bf16[3,128,128]{2,1,0:T(8,128)(2,1)S(1)}, bf16[3,128,128]{2,1,0:T(8,128)(2,1)}, u32[]{:S(2)}) copy-start(bf16[3,128,128]{2,1,0:T(8,128)(2,1)} %param.19) | copy-start | bytes 294916
  30.7 8.4 %copy-start.7 = (bf16[2048,384]{1,0:T(8,128)(2,1)S(1)}, bf16[2048,384]{1,0:T(8,128)(2,1)}, u32[]{:S(2)}) copy-start(bf16[2048,384]{1,0:T(8,128)(2,1)} %param.16) | copy-start | bytes 4718596
  30.7 85.4 %all-to-all-start.1 = ((bf16[8,48,2048]{2,1,0:T(8,128)(2,1)}), bf16[8,48,2048]{2,1,0:T(8,128)(2,1)}, u32[]{:S(2)}, u32[]{:S(2)}) async-start(bf16[8,48,2048]{2,1,0:T(8,128)(2,1)} %bitcast.21), calls=%async_computation.1 | async-start | bytes 3145728 | tf_op jit(solution)/shard_map/all_to_all | solution.py:144
  41.0 2.5 copy-start.12
  120.0 2.9 copy-start.6
  125.0 76.4 %all-to-all-start = ((bf16[8,48,2048]{2,1,0:T(8,128)(2,1)}), bf16[8,48,2048]{2,1,0:T(8,128)(2,1)}, u32[]{:S(2)}, u32[]{:S(2)}) async-start(bf16[8,48,2048]{2,1,0:T(8,128)(2,1)} %bitcast.206), calls=%async_computation | async-start | bytes 3145728 | tf_op jit(solution)/shard_map/all_to_all | solution.py:129
  132.6 184.8 %all-reduce.2.cloned.1.call-start = ((), (), s32[]{:S(2)}) async-start(), calls=%async_computation.3 | async-start | bytes 196608 | tf_op jit(solution)/shard_map/psum | solution.py:160
  144.5 56.8 %copy-start.10 = (s32[384]{0:T(512)S(1)}, s32[384]{0:T(512)}, u32[]{:S(2)}) copy-start(s32[384]{0:T(512)} %copy-done.9) | copy-start | bytes 4612
  201.3 2.6 copy-start.2
  205.2 150.4 %all-gather.2.cloned.1.call-start = ((), (), s32[]{:S(2)}) async-start(), calls=%async_computation.2 | async-start | bytes 1671168 | tf_op jit(solution)/shard_map/all_gather | solution.py:159
  238.9 80.2 %collective-permute-start.2 = (bf16[4,2,3,2,128,128]{4,0,3,5,2,1:T(4,128)(2,1)}, bf16[4,2,3,2,128,128]{4,0,3,5,2,1:T(4,128)(2,1)}, u32[]{:S(2)}, u32[]{:S(2)}) collective-permute-start(bf16[4,2,3,2,128,128]{4,0,3,5,2,1:T(4,128)(2,1)} %get-tuple-element.319), channel_id=1, source_target_pairs={{8,0},{16,8},{24,16},{32,24},{40,32},{48,40},{56,48},{64,56},{72,6... | collective-permute-start | bytes 4718600 | tf_op jit(solution)/shard_map/ppermute | solution.py:30
  240.8 10.7 %copy-start.5 = (bf16[4,3,512,128]{3,2,1,0:T(8,128)(2,1)S(1)}, bf16[4,3,512,128]{3,2,1,0:T(8,128)(2,1)}, u32[]{:S(2)}) copy-start(bf16[4,3,512,128]{3,2,1,0:T(8,128)(2,1)} %get-tuple-element.123) | copy-start | bytes 4718596
  240.8 83.1 %collective-permute-start.3 = (bf16[4,2,3,2,128,128]{4,0,3,5,2,1:T(4,128)(2,1)}, bf16[4,2,3,2,128,128]{4,0,3,5,2,1:T(4,128)(2,1)}, u32[]{:S(2)}, u32[]{:S(2)}) collective-permute-start(bf16[4,2,3,2,128,128]{4,0,3,5,2,1:T(4,128)(2,1)} %get-tuple-element.318), channel_id=1, source_target_pairs={{0,8},{8,16},{16,24},{24,32},{32,40},{40,48},{48,56},{56,64},{64,7... | collective-permute-start | bytes 4718600 | tf_op jit(solution)/shard_map/ppermute | solution.py:30
Sparse Core Ops, SparseCore 0:
  205.3 112.0 all-reduce.1
  319.8 35.7 all-gather.1
